TPU v7x, 32 devices: a whole 2x2x4 slice. The times are simulated.
32 devices in a mesh: groups: 2 (over y), rows: 4 (over z), section: 4 (over x, core).
Axes of the slice: x: 2, y: 2, z: 4, core: 2. Of those that a mesh axis runs over, the one named last changes fastest.
Arguments:
- latent: bfloat16 [8, 16, 16, 768], P('groups', 'rows'), parts along dimension 0, may hold values from -1000 to 1000
- target: bfloat16 [8, 16, 16, 768], P('groups', 'rows'), parts along dimension 0, may hold values from -60 to 60
- expand_weight: bfloat16 [4, 768, 1536], P('section', 'rows'), may hold values from -0.21875 to 0.21875
- expand_bias: float32 [4, 1536], P('section'), may hold values from -2 to 2
- reduce_weight: bfloat16 [4, 1536, 768], P('section', 'rows'), may hold values from -0.15625 to 0.15625
- reduce_bias: float32 [4, 768], P('section'), may hold values from -2 to 2
- depth_kernel: float32 [4, 49, 768], P('section'), may hold values from -0.8 to 0.8
- depth_offset: float32 [4, 768], P('section'), may hold values from -2 to 2
- norm_gain: float32 [4, 768], P('section'), may hold values from 0.1 to 1.9
- norm_shift: float32 [4, 768], P('section'), may hold values from -1.2 to 1.2
- layer_scale: float32 [4, 768], P('section'), may hold values from 0.2 to 0.6
Outputs:
- kernel_gradient: float32 [8, 49, 768], P(('groups', 'section')), parts along dimension 0
- offset_gradient: float32 [8, 768], P(('groups', 'section')), parts along dimension 0
- gain_gradient: float32 [8, 768], P(('groups', 'section')), parts along dimension 0
- shift_gradient: float32 [8, 768], P(('groups', 'section')), parts along dimension 0
- scale_gradient: float32 [8, 768], P(('groups', 'section')), parts along dimension 0
There are 2 independent parts, one for each index of `groups`. A program takes and returns all parts, laid end to end along the dimension named above; an argument that names none is the same for every part. Nothing has to cross between parts.
All inputs are finite; a program needn't handle non-finite values.
Results may differ from a plain program's by a relative error of at most 0.005.
The roundings to bfloat16 on the way count: a program that leaves them out, or rounds other values in their place, can miss the bound.
Values may be sent and summed in bfloat16 or wider, within the bound.
A program may use at most 64 MiB of HBM per device.

v0:
```python
import math
import jax
import jax.numpy as jnp
from jax import lax
from jax.sharding import PartitionSpec as P

KS = 7
EPSILON = 1e-06
SQRT_HALF = 0.7071067811865476
INV_ROOT_TAU = 0.3989422804014327


def shifted(value, axis, steps):
    count = lax.axis_size(axis)
    first, last = (max(0, -steps), min(count, count - steps))
    return lax.ppermute(value, axis, [(source, source + steps) for source in range(first, last)])


def with_halo(block, sides, width):
    for axis, dim in sides:
        count = lax.axis_size(axis)
        forward = [(i, i + 1) for i in range(count - 1)]
        backward = [(target, source) for source, target in forward]
        low = lax.ppermute(
            lax.slice_in_dim(block, block.shape[dim] - width, None, axis=dim), axis, forward
        )
        high = lax.ppermute(lax.slice_in_dim(block, 0, width, axis=dim), axis, backward)
        block = jnp.concatenate([low, block, high], axis=dim)
    return block


def depthwise(padded, kernel, offset, height, breadth):
    summed = jnp.zeros((height, breadth, padded.shape[2]), jnp.float32) + offset
    for row_off in range(KS):
        for col_off in range(KS):
            summed = (
                summed
                + kernel[row_off * KS + col_off]
                * padded[row_off : row_off + height, col_off : col_off + breadth]
            )
    return summed


def depthwise_back(padded_slope, kernel, height, breadth):
    margin = KS // 2
    wide_slope = padded_slope.astype(jnp.float32)
    summed = jnp.zeros((height, breadth, padded_slope.shape[2]), jnp.float32)
    for row_off in range(KS):
        for col_off in range(KS):
            first_row = 2 * margin - row_off
            first_col = 2 * margin - col_off
            summed = (
                summed
                + kernel[row_off * KS + col_off]
                * wide_slope[first_row : first_row + height, first_col : first_col + breadth]
            )
    return summed


def kernel_terms(padded, slope, height, breadth):
    pieces = []
    for row_off in range(KS):
        for col_off in range(KS):
            pieces.append(
                jnp.sum(
                    slope * padded[row_off : row_off + height, col_off : col_off + breadth],
                    axis=(0, 1),
                )
            )
    return jnp.stack(pieces)


def normalize(flat):
    centre = jnp.mean(flat, axis=-1, keepdims=True)
    centred = flat - centre
    variance = jnp.mean(centred * centred, axis=-1, keepdims=True)
    inverse = lax.rsqrt(variance + EPSILON)
    return (centred * inverse, inverse)


def gelu_slope(hidden):
    return (
        0.5 * (1.0 + jax.scipy.special.erf(hidden * SQRT_HALF))
        + hidden * jnp.exp(-0.5 * hidden * hidden) * INV_ROOT_TAU
    )


def contract_last(left, right):
    return lax.dot_general(
        left, right, (((1,), (1,)), ((), ())), preferred_element_type=jnp.float32
    )


def project_forward(mixed, gain, shift, w_expand, b_expand, w_reduce, b_reduce):
    normed, inverse = normalize(mixed)
    inputs = (normed * gain + shift).astype(jnp.bfloat16)
    hidden = jnp.dot(inputs, w_expand, preferred_element_type=jnp.float32) + b_expand
    active = jax.nn.gelu(hidden, approximate=False).astype(jnp.bfloat16)
    branch = jnp.dot(active, w_reduce, preferred_element_type=jnp.float32) + b_reduce
    return (normed, inverse, hidden, branch)


def project_backward(incoming, normed, inverse, hidden, branch, gain, scale, w_expand, w_reduce):
    arrived = incoming.astype(jnp.float32)
    scale_term = jnp.sum(arrived * branch, axis=0)
    reduced = (arrived * scale).astype(jnp.bfloat16)
    spread = contract_last(reduced, w_reduce)
    hidden_slope = (spread * gelu_slope(hidden)).astype(jnp.bfloat16)
    normal_slope = contract_last(hidden_slope, w_expand)
    gain_term = jnp.sum(normal_slope * normed, axis=0)
    shift_term = jnp.sum(normal_slope, axis=0)
    scaled = normal_slope * gain
    slope = (
        scaled
        - jnp.mean(scaled, axis=-1, keepdims=True)
        - normed * jnp.mean(scaled * normed, axis=-1, keepdims=True)
    ) * inverse
    offset_term = jnp.sum(slope, axis=0)
    return (slope, scale_term, gain_term, shift_term, offset_term)


def per_device(
    latent,
    target,
    expand_weight,
    expand_bias,
    reduce_weight,
    reduce_bias,
    depth_kernel,
    depth_offset,
    norm_gain,
    norm_shift,
    layer_scale,
):
    sections = lax.axis_size("section")
    section_pos = lax.axis_index("section")
    micro_count, height, breadth, channels = latent.shape
    margin = KS // 2
    moments = micro_count + sections - 1
    total_rows = height * lax.axis_size("rows")
    loss_scale = 1.0 / math.sqrt(micro_count * total_rows * breadth)
    kernel = depth_kernel[0]
    offset = depth_offset[0]
    gain = norm_gain[0]
    shift = norm_shift[0]
    scale = layer_scale[0]
    b_expand = expand_bias[0]
    b_reduce = reduce_bias[0]
    hidden_units = expand_weight.shape[2]
    tokens = height * breadth
    w_expand, w_reduce = (
        lax.all_gather(expand_weight[0], "rows", axis=0, tiled=True),
        lax.all_gather(reduce_weight[0], "rows", axis=0, tiled=True),
    )
    spare_grid = jnp.zeros((height, breadth, channels), jnp.bfloat16)
    kept = (
        jnp.zeros((micro_count, height + 2 * margin, breadth, channels), jnp.bfloat16),
        jnp.zeros((micro_count, tokens, channels), jnp.float32),
        jnp.zeros((micro_count, height, breadth, channels), jnp.bfloat16),
    )
    kept = kept + (
        jnp.zeros((micro_count, tokens, hidden_units), jnp.float32),
        jnp.zeros((micro_count, tokens, channels), jnp.float32),
    )

    def forward_moment(state_in, moment):
        previous, stores = state_in
        arrived = shifted(previous, "section", 1)
        micro_pos = moment - section_pos
        valid = (micro_pos >= 0) & (micro_pos < micro_count)
        safe_pos = jnp.clip(micro_pos, 0, micro_count - 1)
        fresh = lax.dynamic_index_in_dim(latent, safe_pos, 0, keepdims=False)
        source = jnp.where(section_pos == 0, fresh, arrived)
        framed = with_halo(source, (("rows", 0),), margin)

        def forward_working(buffers):
            padded = jnp.pad(framed.astype(jnp.float32), ((0, 0), (margin, margin), (0, 0)))
            mixed = depthwise(padded, kernel, offset, height, breadth).reshape(tokens, channels)
            normed, inverse, hidden, branch = project_forward(
                mixed, gain, shift, w_expand, b_expand, w_reduce, b_reduce
            )
            output = (
                source.astype(jnp.float32) + scale * branch.reshape(height, breadth, channels)
            ).astype(jnp.bfloat16)
            fresh_items = (framed, mixed, output)
            fresh_items = fresh_items + (hidden, branch)
            updated = tuple(
                (
                    lax.dynamic_update_index_in_dim(buffer, element, safe_pos, 0)
                    for buffer, element in zip(buffers, fresh_items)
                )
            )
            return (output, updated)

        def forward_resting(buffers):
            return (spare_grid, buffers)

        output, stores = lax.cond(valid, forward_working, forward_resting, stores)
        return ((output, stores), None)

    forward_state = lax.scan(forward_moment, (spare_grid, kept), jnp.arange(moments))[0]
    kept = forward_state[1]
    back_expand, back_reduce = (
        lax.all_gather(expand_weight[0], "rows", axis=0, tiled=True),
        lax.all_gather(reduce_weight[0], "rows", axis=0, tiled=True),
    )
    zero_sums = (
        jnp.zeros((KS * KS, channels), jnp.float32),
        jnp.zeros((channels,), jnp.float32),
        jnp.zeros((channels,), jnp.float32),
        jnp.zeros((channels,), jnp.float32),
        jnp.zeros((channels,), jnp.float32),
    )

    def backward_moment(state_in, moment):
        previous, totals = state_in
        arrived = shifted(previous, "section", -1)
        micro_pos = moment - (sections - 1 - section_pos)
        valid = (micro_pos >= 0) & (micro_pos < micro_count)
        safe_pos = jnp.clip(micro_pos, 0, micro_count - 1)
        own_output = lax.dynamic_index_in_dim(kept[2], safe_pos, 0, keepdims=False)
        aimed = lax.dynamic_index_in_dim(target, safe_pos, 0, keepdims=False)
        start_slope = (
            (own_output.astype(jnp.float32) - aimed.astype(jnp.float32)) * loss_scale
        ).astype(jnp.bfloat16)
        incoming = jnp.where(section_pos == sections - 1, start_slope, arrived)

        def backward_working(running):
            framed = lax.dynamic_index_in_dim(kept[0], safe_pos, 0, keepdims=False)
            mixed = lax.dynamic_index_in_dim(kept[1], safe_pos, 0, keepdims=False)
            normed, inverse = normalize(mixed)
            hidden = lax.dynamic_index_in_dim(kept[3], safe_pos, 0, keepdims=False)
            branch = lax.dynamic_index_in_dim(kept[4], safe_pos, 0, keepdims=False)
            slope, scale_term, gain_term, shift_term, offset_term = project_backward(
                incoming.reshape(tokens, channels),
                normed,
                inverse,
                hidden,
                branch,
                gain,
                scale,
                back_expand,
                back_reduce,
            )
            padded = jnp.pad(framed.astype(jnp.float32), ((0, 0), (margin, margin), (0, 0)))
            slope_grid = slope.reshape(height, breadth, channels)
            kernel_term = kernel_terms(padded, slope_grid, height, breadth)
            new_totals = (
                running[0] + kernel_term,
                running[1] + offset_term,
                running[2] + gain_term,
                running[3] + shift_term,
                running[4] + scale_term,
            )
            return (slope_grid.astype(jnp.bfloat16), new_totals)

        def backward_resting(running):
            return (spare_grid, running)

        slope_low, totals = lax.cond(valid, backward_working, backward_resting, totals)
        slope_framed = with_halo(slope_low, (("rows", 0),), margin)
        padded_slope = jnp.pad(slope_framed, ((0, 0), (margin, margin), (0, 0)))
        spread_back = depthwise_back(padded_slope, kernel, height, breadth)
        passed = (incoming.astype(jnp.float32) + spread_back).astype(jnp.bfloat16)
        passed = jnp.where(valid, passed, spare_grid)
        return ((passed, totals), None)

    backward_state = lax.scan(backward_moment, (spare_grid, zero_sums), jnp.arange(moments))[0]
    totals = backward_state[1]
    kernel_sum, offset_sum, gain_sum, shift_sum, scale_sum = lax.psum(
        (totals[0], totals[1], totals[2], totals[3], totals[4]), "rows"
    )
    return (kernel_sum[None], offset_sum[None], gain_sum[None], shift_sum[None], scale_sum[None])


def solution(mesh):
    placed = (
        P("groups", "rows", None, None),
        P("groups", "rows", None, None),
        P("section", "rows", None),
        P("section", None),
        P("section", "rows", None),
        P("section", None),
        P("section", None, None),
        P("section", None),
        P("section", None),
        P("section", None),
        P("section", None),
    )
    return jax.shard_map(
        per_device,
        mesh=mesh,
        in_specs=placed,
        out_specs=(
            P(("groups", "section"), None, None),
            P(("groups", "section"), None),
            P(("groups", "section"), None),
            P(("groups", "section"), None),
            P(("groups", "section"), None),
        ),
        check_vma=False,
    )
```

profile of v0, /device:TPU:0, one launch (start us, length us, event | category | flops | bytes accessed | tf_op | source)
XLA Modules:
  0.0 587.9 jit_solution(4347107190480502940)
XLA Ops:
  10.3 52.5 %all-gather.5.cloned.1.call-done = bf16[1,768,1536]{2,1,0:T(8,128)(2,1)} async-done(((bf16[1,192,1536]{2,1,0:T(8,128)(2,1)}), bf16[1,768,1536]{2,1,0:T(8,128)(2,1)}) %all-gather.5.cloned.1.call-update) | async-done | bytes 2359312 | tf_op jit(solution)/shard_map/all_gather | solution.py:152
  62.8 50.9 %all-gather.7.cloned.1.call-done = bf16[1,1536,768]{2,1,0:T(8,128)(2,1)} async-done(((bf16[1,384,768]{2,1,0:T(8,128)(2,1)}), bf16[1,1536,768]{2,1,0:T(8,128)(2,1)}) %all-gather.7.cloned.1.call-update) | async-done | bytes 2359312 | tf_op jit(solution)/shard_map/all_gather | solution.py:153
  120.1 195.3 %while.44 = (s32[]{:T(128)}, bf16[4,16,768]{2,1,0:T(8,128)(2,1)}, bf16[4,10,16,768]{3,2,1,0:T(8,128)(2,1)}, f32[4,64,768]{2,1,0:T(8,128)}, bf16[4,4,16,768]{3,2,...) while((s32[]{:T(128)}, bf16[4,16,768]{2,1,0:T(8,128)(2,1)}, ...), condition=%wide.region_5.6_spmd, body=%wide.region_0.5_spmd.sunk | while | flops 314400832 | bytes 13684738 | solution.py:201
  132.5 20.0 %conditional.5 = (bf16[4,16,768]{2,1,0:T(8,128)(2,1)}, bf16[4,10,16,768]{3,2,1,0:T(8,128)(2,1)}, f32[4,64,768]{2,1,0:T(8,128)}, bf16[4,4,16,768]{3,2,1,0:T(8,128...) conditional(s32[]{:T(128)} %convert_element_type.155, (bf16[4,10,16,768]{3,2,1,0:T(8,128)(2,1)}, ...), branch_computations={%region_1.1_spmd, %region_2.4_spmd} | conditional | flops 314105920 | bytes 11619766 | solution.py:198
  157.9 5.0 collective-permute-start.2
  164.9 20.1 %conditional.5 = (bf16[4,16,768]{2,1,0:T(8,128)(2,1)}, bf16[4,10,16,768]{3,2,1,0:T(8,128)(2,1)}, f32[4,64,768]{2,1,0:T(8,128)}, bf16[4,4,16,768]{3,2,1,0:T(8,128...) conditional(s32[]{:T(128)} %convert_element_type.155, (bf16[4,10,16,768]{3,2,1,0:T(8,128)(2,1)}, ...), branch_computations={%region_1.1_spmd, %region_2.4_spmd} | conditional | flops 314105920 | bytes 11619766 | solution.py:198
  190.3 4.9 collective-permute-start.2
  197.2 20.0 %conditional.5 = (bf16[4,16,768]{2,1,0:T(8,128)(2,1)}, bf16[4,10,16,768]{3,2,1,0:T(8,128)(2,1)}, f32[4,64,768]{2,1,0:T(8,128)}, bf16[4,4,16,768]{3,2,1,0:T(8,128...) conditional(s32[]{:T(128)} %convert_element_type.155, (bf16[4,10,16,768]{3,2,1,0:T(8,128)(2,1)}, ...), branch_computations={%region_1.1_spmd, %region_2.4_spmd} | conditional | flops 314105920 | bytes 11619766 | solution.py:198
  222.6 4.9 collective-permute-start.2
  229.5 20.0 %conditional.5 = (bf16[4,16,768]{2,1,0:T(8,128)(2,1)}, bf16[4,10,16,768]{3,2,1,0:T(8,128)(2,1)}, f32[4,64,768]{2,1,0:T(8,128)}, bf16[4,4,16,768]{3,2,1,0:T(8,128...) conditional(s32[]{:T(128)} %convert_element_type.155, (bf16[4,10,16,768]{3,2,1,0:T(8,128)(2,1)}, ...), branch_computations={%region_1.1_spmd, %region_2.4_spmd} | conditional | flops 314105920 | bytes 11619766 | solution.py:198
  256.9 4.6 collective-permute-start.2
  264.2 24.0 %collective-permute-start = (bf16[4,16,768]{2,1,0:T(8,128)(2,1)}, bf16[4,16,768]{2,1,0:T(8,128)(2,1)S(1)}, u32[]{:S(2)}, u32[]{:S(2)}) collective-permute-start(bf16[4,16,768]{2,1,0:T(8,128)(2,1)} %get-tuple-element.1363), channel_id=1, source_target_pairs={{0,1},{1,2},{2,3},{4,5},{5,6},{6,7},{8,9},{9,10},{10,11},{12,13},{... | collective-permute-start | bytes 294920 | tf_op jit(solution)/shard_map/while/body/eval_jaxpr/ppermute | solution.py:16
  299.5 4.6 collective-permute-start
  315.5 227.0 %while.45 = (s32[]{:T(128)}, bf16[4,16,768]{2,1,0:T(8,128)(2,1)S(1)}, f32[49,768]{1,0:T(8,128)S(1)}, f32[768]{0:T(1024)S(1)}, f32[768]{0:T(1024)S(1)}, /*index=5...) while((s32[]{:T(128)}, ...), condition=%wide.region_66.67_spmd.clone, body=%wide.region_6.66_spmd.clone.sunk | while | flops 316624960 | bytes 26198456 | solution.py:268
  321.0 19.3 %collective-permute-done.3 = bf16[4,16,768]{2,1,0:T(8,128)(2,1)S(1)} collective-permute-done((bf16[4,16,768]{2,1,0:T(8,128)(2,1)S(1)}, bf16[4,16,768]{2,1,0:T(8,128)(2,1)S(1)}, u32[]{:S(2)}, u32[]{:S(2)}) %collective-permute-start.3) | collective-permute-done | bytes 98336 | tf_op jit(solution)/shard_map/while/body/eval_jaxpr/ppermute | solution.py:16
  373.2 12.3 %collective-permute-done.3 = bf16[4,16,768]{2,1,0:T(8,128)(2,1)S(1)} collective-permute-done((bf16[4,16,768]{2,1,0:T(8,128)(2,1)S(1)}, bf16[4,16,768]{2,1,0:T(8,128)(2,1)S(1)}, u32[]{:S(2)}, u32[]{:S(2)}) %collective-permute-start.3) | collective-permute-done | bytes 98336 | tf_op jit(solution)/shard_map/while/body/eval_jaxpr/ppermute | solution.py:16
  401.4 33.9 %collective-permute-done.3 = bf16[4,16,768]{2,1,0:T(8,128)(2,1)S(1)} collective-permute-done((bf16[4,16,768]{2,1,0:T(8,128)(2,1)S(1)}, bf16[4,16,768]{2,1,0:T(8,128)(2,1)S(1)}, u32[]{:S(2)}, u32[]{:S(2)}) %collective-permute-start.3) | collective-permute-done | bytes 98336 | tf_op jit(solution)/shard_map/while/body/eval_jaxpr/ppermute | solution.py:16
  436.2 11.6 %conditional.6 = (bf16[4,16,768]{2,1,0:T(8,128)(2,1)S(1)}, f32[49,768]{1,0:T(8,128)S(1)}, f32[768]{0:T(1024)S(1)}, f32[768]{0:T(1024)S(1)}, f32[768]{0:T(1024)S(1)}, /*index=5*/f32[768]{0:T(1024)S(1)}) conditional(s32[]{:T(128)} %convert_element_type.162, (f32[49,768]{1,0:T(8,128)S(1)}, f32[768]{0:T(1024)S(1)}, f32[768]{0:T(1024)S(1)}, ...), branch_computations={%region_7.7_spmd, %region_8.65_spmd} | conditional | flops 309289024 | bytes 13126506 | solution.py:260
  464.7 11.6 %conditional.6 = (bf16[4,16,768]{2,1,0:T(8,128)(2,1)S(1)}, f32[49,768]{1,0:T(8,128)S(1)}, f32[768]{0:T(1024)S(1)}, f32[768]{0:T(1024)S(1)}, f32[768]{0:T(1024)S(1)}, /*index=5*/f32[768]{0:T(1024)S(1)}) conditional(s32[]{:T(128)} %convert_element_type.162, (f32[49,768]{1,0:T(8,128)S(1)}, f32[768]{0:T(1024)S(1)}, f32[768]{0:T(1024)S(1)}, ...), branch_computations={%region_7.7_spmd, %region_8.65_spmd} | conditional | flops 309289024 | bytes 13126506 | solution.py:260
  493.3 11.6 %conditional.6 = (bf16[4,16,768]{2,1,0:T(8,128)(2,1)S(1)}, f32[49,768]{1,0:T(8,128)S(1)}, f32[768]{0:T(1024)S(1)}, f32[768]{0:T(1024)S(1)}, f32[768]{0:T(1024)S(1)}, /*index=5*/f32[768]{0:T(1024)S(1)}) conditional(s32[]{:T(128)} %convert_element_type.162, (f32[49,768]{1,0:T(8,128)S(1)}, f32[768]{0:T(1024)S(1)}, f32[768]{0:T(1024)S(1)}, ...), branch_computations={%region_7.7_spmd, %region_8.65_spmd} | conditional | flops 309289024 | bytes 13126506 | solution.py:260
  506.3 4.6 collective-permute-start.5
  521.7 11.6 %conditional.6 = (bf16[4,16,768]{2,1,0:T(8,128)(2,1)S(1)}, f32[49,768]{1,0:T(8,128)S(1)}, f32[768]{0:T(1024)S(1)}, f32[768]{0:T(1024)S(1)}, f32[768]{0:T(1024)S(1)}, /*index=5*/f32[768]{0:T(1024)S(1)}) conditional(s32[]{:T(128)} %convert_element_type.162, (f32[49,768]{1,0:T(8,128)S(1)}, f32[768]{0:T(1024)S(1)}, f32[768]{0:T(1024)S(1)}, ...), branch_computations={%region_7.7_spmd, %region_8.65_spmd} | conditional | flops 309289024 | bytes 13126506 | solution.py:260
  543.4 21.2 %all-reduce.3 = (f32[1,768]{1,0:T(1,128)}, f32[1,768]{1,0:T(1,128)}, f32[1,768]{1,0:T(1,128)}, f32[1,768]{1,0:T(1,128)}) all-reduce(f32[1,768]{1,0:T(1,128)S(1)} %broadcast_in_dim.73, f32[1,768]{1,0:T(1,128)S(1)} %broadcast_in_dim.74, f32[1,768]{1,0:T(1,128)S(1)} %broadcast_in_dim.75, ...), channel_id=1, replica_groups=mesh['groups'=2,'rows'=4,'section'=4] {'rows'}, use_global_device_ids=true, to_apply=%region_68.69 | all-reduce | flops 3072 | bytes 24576 | tf_op jit(solution)/shard_map/psum | solution.py:270
  564.6 15.2 %all-reduce.6.cloned.1.call-done = f32[1,49,768]{2,0,1:T(1,128)} async-done(((f32[1,49,768]{2,0,1:T(1,128)}), f32[1,49,768]{2,0,1:T(1,128)}) %all-reduce.6.cloned.1.call-update) | async-done | bytes 150544 | tf_op jit(solution)/shard_map/psum | solution.py:270
  (590 shorter events, 306.0 us)
Async XLA Ops:
  7.2 55.6 %all-gather.5.cloned.1.call-start = ((), (), s32[]{:S(2)}) async-start(), calls=%async_computation.1 | async-start | bytes 2949120 | tf_op jit(solution)/shard_map/all_gather | solution.py:152
  7.9 105.8 %all-gather.7.cloned.1.call-start = ((), (), s32[]{:S(2)}) async-start(), calls=%async_computation.2 | async-start | bytes 2949120 | tf_op jit(solution)/shard_map/all_gather | solution.py:153
  8.6 571.1 %all-reduce.6.cloned.1.call-start = ((), (), s32[]{:S(2)}) async-start(), calls=%async_computation | async-start | bytes 301056 | tf_op jit(solution)/shard_map/psum | solution.py:270
  125.9 6.6 %collective-permute-start.2 = (bf16[3,16,768]{2,1,0:T(8,128)(2,1)S(1)}, bf16[3,16,768]{2,1,0:T(8,128)(2,1)S(1)}, u32[]{:S(2)}, u32[]{:S(2)}) collective-permute-start(bf16[3,16,768]{2,1,0:T(8,128)(2,1)S(1)} %get-tuple-element.1229), channel_id=1, source_target_pairs={{0,4},{4,8},{8,12},{1,5},{5,9},{9,13},{2,6},{6,10},{10,14},{3,7},{... | collective-permute-start | bytes 221192 | tf_op jit(solution)/shard_map/while/body/eval_jaxpr/ppermute | solution.py:24
  156.6 6.7 %collective-permute-start.1 = (bf16[3,16,768]{2,1,0:T(8,128)(2,1)S(1)}, bf16[3,16,768]{2,1,0:T(8,128)(2,1)S(1)}, u32[]{:S(2)}, u32[]{:S(2)}) collective-permute-start(bf16[3,16,768]{2,1,0:T(8,128)(2,1)S(1)} %get-tuple-element.1228), channel_id=1, source_target_pairs={{4,0},{8,4},{12,8},{5,1},{9,5},{13,9},{6,2},{10,6},{14,10},{7,3},{... | collective-permute-start | bytes 221192 | tf_op jit(solution)/shard_map/while/body/eval_jaxpr/ppermute | solution.py:27
  157.9 7.0 %collective-permute-start.2 = (bf16[3,16,768]{2,1,0:T(8,128)(2,1)S(1)}, bf16[3,16,768]{2,1,0:T(8,128)(2,1)S(1)}, u32[]{:S(2)}, u32[]{:S(2)}) collective-permute-start(bf16[3,16,768]{2,1,0:T(8,128)(2,1)S(1)} %get-tuple-element.1229), channel_id=1, source_target_pairs={{0,4},{4,8},{8,12},{1,5},{5,9},{9,13},{2,6},{6,10},{10,14},{3,7},{... | collective-permute-start | bytes 221192 | tf_op jit(solution)/shard_map/while/body/eval_jaxpr/ppermute | solution.py:24
  189.0 6.6 %collective-permute-start.1 = (bf16[3,16,768]{2,1,0:T(8,128)(2,1)S(1)}, bf16[3,16,768]{2,1,0:T(8,128)(2,1)S(1)}, u32[]{:S(2)}, u32[]{:S(2)}) collective-permute-start(bf16[3,16,768]{2,1,0:T(8,128)(2,1)S(1)} %get-tuple-element.1228), channel_id=1, source_target_pairs={{4,0},{8,4},{12,8},{5,1},{9,5},{13,9},{6,2},{10,6},{14,10},{7,3},{... | collective-permute-start | bytes 221192 | tf_op jit(solution)/shard_map/while/body/eval_jaxpr/ppermute | solution.py:27
  190.3 6.9 %collective-permute-start.2 = (bf16[3,16,768]{2,1,0:T(8,128)(2,1)S(1)}, bf16[3,16,768]{2,1,0:T(8,128)(2,1)S(1)}, u32[]{:S(2)}, u32[]{:S(2)}) collective-permute-start(bf16[3,16,768]{2,1,0:T(8,128)(2,1)S(1)} %get-tuple-element.1229), channel_id=1, source_target_pairs={{0,4},{4,8},{8,12},{1,5},{5,9},{9,13},{2,6},{6,10},{10,14},{3,7},{... | collective-permute-start | bytes 221192 | tf_op jit(solution)/shard_map/while/body/eval_jaxpr/ppermute | solution.py:24
  221.3 6.6 %collective-permute-start.1 = (bf16[3,16,768]{2,1,0:T(8,128)(2,1)S(1)}, bf16[3,16,768]{2,1,0:T(8,128)(2,1)S(1)}, u32[]{:S(2)}, u32[]{:S(2)}) collective-permute-start(bf16[3,16,768]{2,1,0:T(8,128)(2,1)S(1)} %get-tuple-element.1228), channel_id=1, source_target_pairs={{4,0},{8,4},{12,8},{5,1},{9,5},{13,9},{6,2},{10,6},{14,10},{7,3},{... | collective-permute-start | bytes 221192 | tf_op jit(solution)/shard_map/while/body/eval_jaxpr/ppermute | solution.py:27
  222.6 6.9 %collective-permute-start.2 = (bf16[3,16,768]{2,1,0:T(8,128)(2,1)S(1)}, bf16[3,16,768]{2,1,0:T(8,128)(2,1)S(1)}, u32[]{:S(2)}, u32[]{:S(2)}) collective-permute-start(bf16[3,16,768]{2,1,0:T(8,128)(2,1)S(1)} %get-tuple-element.1229), channel_id=1, source_target_pairs={{0,4},{4,8},{8,12},{1,5},{5,9},{9,13},{2,6},{6,10},{10,14},{3,7},{... | collective-permute-start | bytes 221192 | tf_op jit(solution)/shard_map/while/body/eval_jaxpr/ppermute | solution.py:24
  264.2 25.8 %collective-permute-start = (bf16[4,16,768]{2,1,0:T(8,128)(2,1)}, bf16[4,16,768]{2,1,0:T(8,128)(2,1)S(1)}, u32[]{:S(2)}, u32[]{:S(2)}) collective-permute-start(bf16[4,16,768]{2,1,0:T(8,128)(2,1)} %get-tuple-element.1363), channel_id=1, source_target_pairs={{0,1},{1,2},{2,3},{4,5},{5,6},{6,7},{8,9},{9,10},{10,11},{12,13},{... | collective-permute-start | bytes 294920 | tf_op jit(solution)/shard_map/while/body/eval_jaxpr/ppermute | solution.py:16
  315.5 24.8 %collective-permute-start.3 = (bf16[4,16,768]{2,1,0:T(8,128)(2,1)S(1)}, bf16[4,16,768]{2,1,0:T(8,128)(2,1)S(1)}, u32[]{:S(2)}, u32[]{:S(2)}) collective-permute-start(bf16[4,16,768]{2,1,0:T(8,128)(2,1)S(1)} %broadcast_select_fusion.4), channel_id=1, source_target_pairs={{1,0},{2,1},{3,2},{5,4},{6,5},{7,6},{9,8},{10,9},{11,10},{13,12},{... | collective-permute-start | bytes 294920 | tf_op jit(solution)/shard_map/while/body/eval_jaxpr/ppermute | solution.py:16
  341.4 7.1 %collective-permute-start.4 = (bf16[3,16,768]{2,1,0:T(8,128)(2,1)S(1)}, bf16[3,16,768]{2,1,0:T(8,128)(2,1)S(1)}, u32[]{:S(2)}, u32[]{:S(2)}) collective-permute-start(bf16[3,16,768]{2,1,0:T(8,128)(2,1)S(1)} %get-tuple-element.1258), channel_id=1, source_target_pairs={{4,0},{8,4},{12,8},{5,1},{9,5},{13,9},{6,2},{10,6},{14,10},{7,3},{... | collective-permute-start | bytes 221192 | tf_op jit(solution)/shard_map/while/body/eval_jaxpr/ppermute | solution.py:27
  350.6 6.8 %collective-permute-start.3 = (bf16[4,16,768]{2,1,0:T(8,128)(2,1)S(1)}, bf16[4,16,768]{2,1,0:T(8,128)(2,1)S(1)}, u32[]{:S(2)}, u32[]{:S(2)}) collective-permute-start(bf16[4,16,768]{2,1,0:T(8,128)(2,1)S(1)} %broadcast_select_fusion.4), channel_id=1, source_target_pairs={{1,0},{2,1},{3,2},{5,4},{6,5},{7,6},{9,8},{10,9},{11,10},{13,12},{... | collective-permute-start | bytes 294920 | tf_op jit(solution)/shard_map/while/body/eval_jaxpr/ppermute | solution.py:16
  358.5 7.1 %collective-permute-start.4 = (bf16[3,16,768]{2,1,0:T(8,128)(2,1)S(1)}, bf16[3,16,768]{2,1,0:T(8,128)(2,1)S(1)}, u32[]{:S(2)}, u32[]{:S(2)}) collective-permute-start(bf16[3,16,768]{2,1,0:T(8,128)(2,1)S(1)} %get-tuple-element.1258), channel_id=1, source_target_pairs={{4,0},{8,4},{12,8},{5,1},{9,5},{13,9},{6,2},{10,6},{14,10},{7,3},{... | collective-permute-start | bytes 221192 | tf_op jit(solution)/shard_map/while/body/eval_jaxpr/ppermute | solution.py:27
  367.7 17.8 %collective-permute-start.3 = (bf16[4,16,768]{2,1,0:T(8,128)(2,1)S(1)}, bf16[4,16,768]{2,1,0:T(8,128)(2,1)S(1)}, u32[]{:S(2)}, u32[]{:S(2)}) collective-permute-start(bf16[4,16,768]{2,1,0:T(8,128)(2,1)S(1)} %broadcast_select_fusion.4), channel_id=1, source_target_pairs={{1,0},{2,1},{3,2},{5,4},{6,5},{7,6},{9,8},{10,9},{11,10},{13,12},{... | collective-permute-start | bytes 294920 | tf_op jit(solution)/shard_map/while/body/eval_jaxpr/ppermute | solution.py:16
  386.6 7.1 %collective-permute-start.4 = (bf16[3,16,768]{2,1,0:T(8,128)(2,1)S(1)}, bf16[3,16,768]{2,1,0:T(8,128)(2,1)S(1)}, u32[]{:S(2)}, u32[]{:S(2)}) collective-permute-start(bf16[3,16,768]{2,1,0:T(8,128)(2,1)S(1)} %get-tuple-element.1258), channel_id=1, source_target_pairs={{4,0},{8,4},{12,8},{5,1},{9,5},{13,9},{6,2},{10,6},{14,10},{7,3},{... | collective-permute-start | bytes 221192 | tf_op jit(solution)/shard_map/while/body/eval_jaxpr/ppermute | solution.py:27
  395.9 39.4 %collective-permute-start.3 = (bf16[4,16,768]{2,1,0:T(8,128)(2,1)S(1)}, bf16[4,16,768]{2,1,0:T(8,128)(2,1)S(1)}, u32[]{:S(2)}, u32[]{:S(2)}) collective-permute-start(bf16[4,16,768]{2,1,0:T(8,128)(2,1)S(1)} %broadcast_select_fusion.4), channel_id=1, source_target_pairs={{1,0},{2,1},{3,2},{5,4},{6,5},{7,6},{9,8},{10,9},{11,10},{13,12},{... | collective-permute-start | bytes 294920 | tf_op jit(solution)/shard_map/while/body/eval_jaxpr/ppermute | solution.py:16
  447.9 7.1 %collective-permute-start.4 = (bf16[3,16,768]{2,1,0:T(8,128)(2,1)S(1)}, bf16[3,16,768]{2,1,0:T(8,128)(2,1)S(1)}, u32[]{:S(2)}, u32[]{:S(2)}) collective-permute-start(bf16[3,16,768]{2,1,0:T(8,128)(2,1)S(1)} %get-tuple-element.1258), channel_id=1, source_target_pairs={{4,0},{8,4},{12,8},{5,1},{9,5},{13,9},{6,2},{10,6},{14,10},{7,3},{... | collective-permute-start | bytes 221192 | tf_op jit(solution)/shard_map/while/body/eval_jaxpr/ppermute | solution.py:27
  476.3 7.1 %collective-permute-start.4 = (bf16[3,16,768]{2,1,0:T(8,128)(2,1)S(1)}, bf16[3,16,768]{2,1,0:T(8,128)(2,1)S(1)}, u32[]{:S(2)}, u32[]{:S(2)}) collective-permute-start(bf16[3,16,768]{2,1,0:T(8,128)(2,1)S(1)} %get-tuple-element.1258), channel_id=1, source_target_pairs={{4,0},{8,4},{12,8},{5,1},{9,5},{13,9},{6,2},{10,6},{14,10},{7,3},{... | collective-permute-start | bytes 221192 | tf_op jit(solution)/shard_map/while/body/eval_jaxpr/ppermute | solution.py:27
  485.6 6.7 %collective-permute-start.3 = (bf16[4,16,768]{2,1,0:T(8,128)(2,1)S(1)}, bf16[4,16,768]{2,1,0:T(8,128)(2,1)S(1)}, u32[]{:S(2)}, u32[]{:S(2)}) collective-permute-start(bf16[4,16,768]{2,1,0:T(8,128)(2,1)S(1)} %broadcast_select_fusion.4), channel_id=1, source_target_pairs={{1,0},{2,1},{3,2},{5,4},{6,5},{7,6},{9,8},{10,9},{11,10},{13,12},{... | collective-permute-start | bytes 294920 | tf_op jit(solution)/shard_map/while/body/eval_jaxpr/ppermute | solution.py:16
  505.0 7.1 %collective-permute-start.4 = (bf16[3,16,768]{2,1,0:T(8,128)(2,1)S(1)}, bf16[3,16,768]{2,1,0:T(8,128)(2,1)S(1)}, u32[]{:S(2)}, u32[]{:S(2)}) collective-permute-start(bf16[3,16,768]{2,1,0:T(8,128)(2,1)S(1)} %get-tuple-element.1258), channel_id=1, source_target_pairs={{4,0},{8,4},{12,8},{5,1},{9,5},{13,9},{6,2},{10,6},{14,10},{7,3},{... | collective-permute-start | bytes 221192 | tf_op jit(solution)/shard_map/while/body/eval_jaxpr/ppermute | solution.py:27
  506.3 6.6 %collective-permute-start.5 = (bf16[3,16,768]{2,1,0:T(8,128)(2,1)S(1)}, bf16[3,16,768]{2,1,0:T(8,128)(2,1)S(1)}, u32[]{:S(2)}, u32[]{:S(2)}) collective-permute-start(bf16[3,16,768]{2,1,0:T(8,128)(2,1)S(1)} %get-tuple-element.1259), channel_id=1, source_target_pairs={{0,4},{4,8},{8,12},{1,5},{5,9},{9,13},{2,6},{6,10},{10,14},{3,7},{... | collective-permute-start | bytes 221192 | tf_op jit(solution)/shard_map/while/body/eval_jaxpr/ppermute | solution.py:24
  533.3 7.1 %collective-permute-start.4 = (bf16[3,16,768]{2,1,0:T(8,128)(2,1)S(1)}, bf16[3,16,768]{2,1,0:T(8,128)(2,1)S(1)}, u32[]{:S(2)}, u32[]{:S(2)}) collective-permute-start(bf16[3,16,768]{2,1,0:T(8,128)(2,1)S(1)} %get-tuple-element.1258), channel_id=1, source_target_pairs={{4,0},{8,4},{12,8},{5,1},{9,5},{13,9},{6,2},{10,6},{14,10},{7,3},{... | collective-permute-start | bytes 221192 | tf_op jit(solution)/shard_map/while/body/eval_jaxpr/ppermute | solution.py:27
  (30 other events, 209.3 us)
Sparse Core Ops, SparseCore 0:
  9.6 53.1 all-gather.4
  64.4 49.2 all-gather.6
  543.4 36.2 all-reduce.5
where the time goes:
time: 595 us; the launch traced here: 588 us
  waiting for transfers between devices  209 us (35%)
  starting transfers between devices  130 us (22%)
  local copies, waits for them, and re-layouts  86.1 us (14%)
  other arithmetic  81.1 us (14%)
  matrix products  33.8 us (6%)
  blocking collectives  21.2 us (4%)
  between operations  13.8 us (2%)
  loops' own time  12.3 us (2%)
    ppermute x14, waiting for transfers between devices, shifted(): lax.ppermute(value, axis, [(source, source + steps) for source in range(f...  70.1 us
    ppermute x14, starting transfers between devices, with_halo(): lax.ppermute(lax.slice_in_dim(block, block.shape[dim] - width, None, axis...  65.5 us
    all_gather x1, waiting for transfers between devices, per_device(): lax.all_gather(expand_weight[0], 'rows', axis=0, tiled=True)  52.5 us
    all_gather x1, waiting for transfers between devices, per_device(): lax.all_gather(reduce_weight[0], 'rows', axis=0, tiled=True)  50.9 us
    ppermute x14, starting transfers between devices, shifted(): lax.ppermute(value, axis, [(source, source + steps) for source in range(f...  46.5 us
    slice x21, local copies, waits for them, and re-layouts, depthwise_back(): kernel[row_off * KS + col_off]  28.6 us
    slice x12, local copies, waits for them, and re-layouts, depthwise(): kernel[row_off * KS + col_off]  23.8 us
    psum x1, blocking collectives, per_device(): lax.psum((totals[0], totals[1], totals[2], totals[3], totals[4]), 'rows')  21.2 us
  transfers between devices with their start and end apart: 45, of which 31 were waited for; matrix products, arithmetic and copies ran while one was open for 7% of the time, Pallas kernels for 0%

commit v1 on v0

--- a/solution.py
+++ b/solution.py
@@ -1,3 +1,4 @@
+import functools
 import math
 import jax
 import jax.numpy as jnp
@@ -8,6 +9,41 @@
 EPSILON = 1e-06
 SQRT_HALF = 0.7071067811865476
 INV_ROOT_TAU = 0.3989422804014327
+
+
+def _push_kinds(mat, axis_id):
+    row_out = lax.axis_size(axis_id)
+    w2, state_next, frame_out = (row_out, lax.axis_index(axis_id), mat.shape[0])
+    arrivals = []
+    u = 0
+    while u < w2:
+        arrivals.append((u, (u + 1) % w2))
+        u = u + 1
+    all_rows = []
+    u = 0
+    while u < w2:
+        all_rows.append((u, (u - 1) % w2))
+        u += 1
+    ready = jnp.zeros((*mat.shape[:0], w2 * frame_out, *mat.shape[1:]), mat.dtype)
+    ready = lax.dynamic_update_slice_in_dim(ready, mat, state_next * frame_out, axis=0)
+    near = part_now = mat
+    z_new = w2 // 2
+    dd = 1
+    while dd < z_new + 1:
+        near = lax.ppermute(near, axis_id, arrivals)
+        ready = lax.dynamic_update_slice_in_dim(
+            ready, near, (state_next - dd) % w2 * frame_out, axis=0
+        )
+        if dd < w2 - z_new:
+            part_now = lax.ppermute(part_now, axis_id, all_rows)
+            ready = lax.dynamic_update_slice_in_dim(
+                ready, part_now, (state_next + dd) % w2 * frame_out, axis=0
+            )
+        dd = dd + 1
+    return ready
+
+
+push_cycles = functools.partial(_push_kinds, axis_id="rows")
 
 
 def shifted(value, axis, steps):
@@ -150,7 +186,7 @@
     tokens = height * breadth
     w_expand, w_reduce = (
         lax.all_gather(expand_weight[0], "rows", axis=0, tiled=True),
-        lax.all_gather(reduce_weight[0], "rows", axis=0, tiled=True),
+        push_cycles(reduce_weight[0]),
     )
     spare_grid = jnp.zeros((height, breadth, channels), jnp.bfloat16)
     kept = (

time: 595 us -> 574 us (0.965)
  waiting for transfers between devices: 209 us -> 168 us
  starting transfers between devices: 130 us -> 146 us
    ppermute x0 -> x3, waiting for transfers between devices: none -> 52.6 us  [the longest x1 29.3 us: _push_kinds(): part_now = lax.ppermute(part_now, axis_id, all_rows)]
    all_gather x1, waiting for transfers between devices: 50.9 us -> 0.01 us  [per_device(): lax.all_gather(reduce_weight[0], 'rows', axis=0, tiled=True)]
    all_gather x1, waiting for transfers between devices: 52.5 us -> 7.66 us  [per_device(): lax.all_gather(expand_weight[0], 'rows', axis=0, tiled=True)]
    ppermute x0 -> x3, starting transfers between devices: none -> 15.4 us  [the longest x2 13.3 us: _push_kinds(): near = lax.ppermute(near, axis_id, arrivals)]
  transfers between devices with their start and end apart: 45 -> 48, of which waited for: 31 -> 32; matrix products, arithmetic and copies ran while one was open for 7% -> 25% of each run, Pallas kernels for 0% -> 0%
where the time goes in v1:
time: 574 us; the launch traced here: 567 us
  waiting for transfers between devices  168 us (29%)
  starting transfers between devices  146 us (25%)
  local copies, waits for them, and re-layouts  90.1 us (16%)
  other arithmetic  81.1 us (14%)
  matrix products  33.8 us (6%)
  blocking collectives  21.3 us (4%)
  between operations  13.9 us (2%)
  loops' own time  12.2 us (2%)
    ppermute x14, waiting for transfers between devices, shifted(): lax.ppermute(value, axis, [(source, source + steps) for source in range(f...  70.5 us
    ppermute x14, starting transfers between devices, with_halo(): lax.ppermute(lax.slice_in_dim(block, block.shape[dim] - width, None, axis...  65.2 us
    ppermute x14, starting transfers between devices, shifted(): lax.ppermute(value, axis, [(source, source + steps) for source in range(f...  47 us
    ppermute x1, waiting for transfers between devices, _push_kinds(): part_now = lax.ppermute(part_now, axis_id, all_rows)  29.3 us
    slice x21, local copies, waits for them, and re-layouts, depthwise_back(): kernel[row_off * KS + col_off]  27.9 us
    slice x12, local copies, waits for them, and re-layouts, depthwise(): kernel[row_off * KS + col_off]  23.6 us
    ppermute x2, waiting for transfers between devices, _push_kinds(): near = lax.ppermute(near, axis_id, arrivals)  23.3 us
    psum x1, blocking collectives, per_device(): lax.psum((totals[0], totals[1], totals[2], totals[3], totals[4]), 'rows')  21.3 us
  transfers between devices with their start and end apart: 48, of which 32 were waited for; matrix products, arithmetic and copies ran while one was open for 25% of the time, Pallas kernels for 0%

profile of v1, /device:TPU:0, one launch (start us, length us, event | category | flops | bytes accessed | tf_op | source)
XLA Modules:
  0.0 566.6 jit_solution(15437609279000571600)
XLA Ops:
  13.1 17.2 %collective-permute-done.6 = bf16[384,768]{1,0:T(8,128)(2,1)} collective-permute-done((bf16[384,768]{1,0:T(8,128)(2,1)}, bf16[384,768]{1,0:T(8,128)(2,1)}, u32[]{:S(2)}, u32[]{:S(2)}) %collective-permute-start.6) | collective-permute-done | bytes 589856 | tf_op jit(solution)/shard_map/ppermute | solution.py:33
  30.3 10.2 %collective-permute-start.8 = (bf16[384,768]{1,0:T(8,128)(2,1)}, bf16[384,768]{1,0:T(8,128)(2,1)}, u32[]{:S(2)}, u32[]{:S(2)}) collective-permute-start(bf16[384,768]{1,0:T(8,128)(2,1)} %collective-permute-done.6), channel_id=1, source_target_pairs={{0,4},{4,8},{8,12},{12,0},{1,5},{5,9},{9,13},{13,1},{2,6},{6,10},{... | collective-permute-start | bytes 1769480 | tf_op jit(solution)/shard_map/ppermute | solution.py:33
  43.5 29.3 %collective-permute-done.7 = bf16[384,768]{1,0:T(8,128)(2,1)} collective-permute-done((bf16[384,768]{1,0:T(8,128)(2,1)}, bf16[384,768]{1,0:T(8,128)(2,1)}, u32[]{:S(2)}, u32[]{:S(2)}) %collective-permute-start.7) | collective-permute-done | bytes 589856 | tf_op jit(solution)/shard_map/ppermute | solution.py:38
  73.9 6.2 %collective-permute-done.8 = bf16[384,768]{1,0:T(8,128)(2,1)} collective-permute-done((bf16[384,768]{1,0:T(8,128)(2,1)}, bf16[384,768]{1,0:T(8,128)(2,1)}, u32[]{:S(2)}, u32[]{:S(2)}) %collective-permute-start.8) | collective-permute-done | bytes 589856 | tf_op jit(solution)/shard_map/ppermute | solution.py:33
  82.6 7.7 %all-gather.5.cloned.1.call-done = bf16[1,768,1536]{2,1,0:T(8,128)(2,1)} async-done(((bf16[1,192,1536]{2,1,0:T(8,128)(2,1)}), bf16[1,768,1536]{2,1,0:T(8,128)(2,1)}) %all-gather.5.cloned.1.call-update) | async-done | bytes 2359312 | tf_op jit(solution)/shard_map/all_gather | solution.py:188
  96.6 197.6 %while.44 = (s32[]{:T(128)}, bf16[4,16,768]{2,1,0:T(8,128)(2,1)}, bf16[4,10,16,768]{3,2,1,0:T(8,128)(2,1)}, f32[4,64,768]{2,1,0:T(8,128)}, bf16[4,4,16,768]{3,2,...) while((s32[]{:T(128)}, bf16[4,16,768]{2,1,0:T(8,128)(2,1)}, ...), condition=%wide.region_5.6_spmd, body=%wide.region_0.5_spmd.sunk | while | flops 314400832 | bytes 13684738 | solution.py:237
  111.6 20.0 %conditional.5 = (bf16[4,16,768]{2,1,0:T(8,128)(2,1)}, bf16[4,10,16,768]{3,2,1,0:T(8,128)(2,1)}, f32[4,64,768]{2,1,0:T(8,128)}, bf16[4,4,16,768]{3,2,1,0:T(8,128...) conditional(s32[]{:T(128)} %convert_element_type.155, (bf16[4,10,16,768]{3,2,1,0:T(8,128)(2,1)}, ...), branch_computations={%region_1.1_spmd, %region_2.4_spmd} | conditional | flops 314105920 | bytes 11619766 | solution.py:234
  136.9 4.7 collective-permute-start.2
  143.6 20.0 %conditional.5 = (bf16[4,16,768]{2,1,0:T(8,128)(2,1)}, bf16[4,10,16,768]{3,2,1,0:T(8,128)(2,1)}, f32[4,64,768]{2,1,0:T(8,128)}, bf16[4,4,16,768]{3,2,1,0:T(8,128...) conditional(s32[]{:T(128)} %convert_element_type.155, (bf16[4,10,16,768]{3,2,1,0:T(8,128)(2,1)}, ...), branch_computations={%region_1.1_spmd, %region_2.4_spmd} | conditional | flops 314105920 | bytes 11619766 | solution.py:234
  168.9 5.0 collective-permute-start.2
  175.8 20.0 %conditional.5 = (bf16[4,16,768]{2,1,0:T(8,128)(2,1)}, bf16[4,10,16,768]{3,2,1,0:T(8,128)(2,1)}, f32[4,64,768]{2,1,0:T(8,128)}, bf16[4,4,16,768]{3,2,1,0:T(8,128...) conditional(s32[]{:T(128)} %convert_element_type.155, (bf16[4,10,16,768]{3,2,1,0:T(8,128)(2,1)}, ...), branch_computations={%region_1.1_spmd, %region_2.4_spmd} | conditional | flops 314105920 | bytes 11619766 | solution.py:234
  201.1 4.9 collective-permute-start.2
  208.0 20.0 %conditional.5 = (bf16[4,16,768]{2,1,0:T(8,128)(2,1)}, bf16[4,10,16,768]{3,2,1,0:T(8,128)(2,1)}, f32[4,64,768]{2,1,0:T(8,128)}, bf16[4,4,16,768]{3,2,1,0:T(8,128...) conditional(s32[]{:T(128)} %convert_element_type.155, (bf16[4,10,16,768]{3,2,1,0:T(8,128)(2,1)}, ...), branch_computations={%region_1.1_spmd, %region_2.4_spmd} | conditional | flops 314105920 | bytes 11619766 | solution.py:234
  243.0 24.0 %collective-permute-start = (bf16[4,16,768]{2,1,0:T(8,128)(2,1)}, bf16[4,16,768]{2,1,0:T(8,128)(2,1)S(1)}, u32[]{:S(2)}, u32[]{:S(2)}) collective-permute-start(bf16[4,16,768]{2,1,0:T(8,128)(2,1)} %get-tuple-element.1363), channel_id=1, source_target_pairs={{0,1},{1,2},{2,3},{4,5},{5,6},{6,7},{8,9},{9,10},{10,11},{12,13},{... | collective-permute-start | bytes 294920 | tf_op jit(solution)/shard_map/while/body/eval_jaxpr/ppermute | solution.py:52
  294.2 226.8 %while.45 = (s32[]{:T(128)}, bf16[4,16,768]{2,1,0:T(8,128)(2,1)S(1)}, f32[49,768]{1,0:T(8,128)S(1)}, f32[768]{0:T(1024)S(1)}, f32[768]{0:T(1024)S(1)}, /*index=5...) while((s32[]{:T(128)}, ...), condition=%wide.region_66.67_spmd.clone, body=%wide.region_6.66_spmd.clone.sunk | while | flops 316624960 | bytes 26198456 | solution.py:304
  299.7 19.4 %collective-permute-done.3 = bf16[4,16,768]{2,1,0:T(8,128)(2,1)S(1)} collective-permute-done((bf16[4,16,768]{2,1,0:T(8,128)(2,1)S(1)}, bf16[4,16,768]{2,1,0:T(8,128)(2,1)S(1)}, u32[]{:S(2)}, u32[]{:S(2)}) %collective-permute-start.3) | collective-permute-done | bytes 98336 | tf_op jit(solution)/shard_map/while/body/eval_jaxpr/ppermute | solution.py:52
  351.9 12.4 %collective-permute-done.3 = bf16[4,16,768]{2,1,0:T(8,128)(2,1)S(1)} collective-permute-done((bf16[4,16,768]{2,1,0:T(8,128)(2,1)S(1)}, bf16[4,16,768]{2,1,0:T(8,128)(2,1)S(1)}, u32[]{:S(2)}, u32[]{:S(2)}) %collective-permute-start.3) | collective-permute-done | bytes 98336 | tf_op jit(solution)/shard_map/while/body/eval_jaxpr/ppermute | solution.py:52
  380.1 33.9 %collective-permute-done.3 = bf16[4,16,768]{2,1,0:T(8,128)(2,1)S(1)} collective-permute-done((bf16[4,16,768]{2,1,0:T(8,128)(2,1)S(1)}, bf16[4,16,768]{2,1,0:T(8,128)(2,1)S(1)}, u32[]{:S(2)}, u32[]{:S(2)}) %collective-permute-start.3) | collective-permute-done | bytes 98336 | tf_op jit(solution)/shard_map/while/body/eval_jaxpr/ppermute | solution.py:52
  414.9 11.6 %conditional.6 = (bf16[4,16,768]{2,1,0:T(8,128)(2,1)S(1)}, f32[49,768]{1,0:T(8,128)S(1)}, f32[768]{0:T(1024)S(1)}, f32[768]{0:T(1024)S(1)}, f32[768]{0:T(1024)S(1)}, /*index=5*/f32[768]{0:T(1024)S(1)}) conditional(s32[]{:T(128)} %convert_element_type.162, (f32[49,768]{1,0:T(8,128)S(1)}, f32[768]{0:T(1024)S(1)}, f32[768]{0:T(1024)S(1)}, ...), branch_computations={%region_7.7_spmd, %region_8.65_spmd} | conditional | flops 309289024 | bytes 13126506 | solution.py:296
  443.4 11.6 %conditional.6 = (bf16[4,16,768]{2,1,0:T(8,128)(2,1)S(1)}, f32[49,768]{1,0:T(8,128)S(1)}, f32[768]{0:T(1024)S(1)}, f32[768]{0:T(1024)S(1)}, f32[768]{0:T(1024)S(1)}, /*index=5*/f32[768]{0:T(1024)S(1)}) conditional(s32[]{:T(128)} %convert_element_type.162, (f32[49,768]{1,0:T(8,128)S(1)}, f32[768]{0:T(1024)S(1)}, f32[768]{0:T(1024)S(1)}, ...), branch_computations={%region_7.7_spmd, %region_8.65_spmd} | conditional | flops 309289024 | bytes 13126506 | solution.py:296
  472.0 11.6 %conditional.6 = (bf16[4,16,768]{2,1,0:T(8,128)(2,1)S(1)}, f32[49,768]{1,0:T(8,128)S(1)}, f32[768]{0:T(1024)S(1)}, f32[768]{0:T(1024)S(1)}, f32[768]{0:T(1024)S(1)}, /*index=5*/f32[768]{0:T(1024)S(1)}) conditional(s32[]{:T(128)} %convert_element_type.162, (f32[49,768]{1,0:T(8,128)S(1)}, f32[768]{0:T(1024)S(1)}, f32[768]{0:T(1024)S(1)}, ...), branch_computations={%region_7.7_spmd, %region_8.65_spmd} | conditional | flops 309289024 | bytes 13126506 | solution.py:296
  500.2 11.6 %conditional.6 = (bf16[4,16,768]{2,1,0:T(8,128)(2,1)S(1)}, f32[49,768]{1,0:T(8,128)S(1)}, f32[768]{0:T(1024)S(1)}, f32[768]{0:T(1024)S(1)}, f32[768]{0:T(1024)S(1)}, /*index=5*/f32[768]{0:T(1024)S(1)}) conditional(s32[]{:T(128)} %convert_element_type.162, (f32[49,768]{1,0:T(8,128)S(1)}, f32[768]{0:T(1024)S(1)}, f32[768]{0:T(1024)S(1)}, ...), branch_computations={%region_7.7_spmd, %region_8.65_spmd} | conditional | flops 309289024 | bytes 13126506 | solution.py:296
  521.9 21.3 %all-reduce.3 = (f32[1,768]{1,0:T(1,128)}, f32[1,768]{1,0:T(1,128)}, f32[1,768]{1,0:T(1,128)}, f32[1,768]{1,0:T(1,128)}) all-reduce(f32[1,768]{1,0:T(1,128)S(1)} %broadcast_in_dim.77, f32[1,768]{1,0:T(1,128)S(1)} %broadcast_in_dim.78, f32[1,768]{1,0:T(1,128)S(1)} %broadcast_in_dim.79, ...), channel_id=1, replica_groups=mesh['groups'=2,'rows'=4,'section'=4] {'rows'}, use_global_device_ids=true, to_apply=%region_68.69 | all-reduce | flops 3072 | bytes 24576 | tf_op jit(solution)/shard_map/psum | solution.py:306
  543.2 15.2 %all-reduce.6.cloned.1.call-done = f32[1,49,768]{2,0,1:T(1,128)} async-done(((f32[1,49,768]{2,0,1:T(1,128)}), f32[1,49,768]{2,0,1:T(1,128)}) %all-reduce.6.cloned.1.call-update) | async-done | bytes 150544 | tf_op jit(solution)/shard_map/psum | solution.py:306
  (605 shorter events, 331.3 us)
Async XLA Ops:
  7.2 83.0 %all-gather.5.cloned.1.call-start = ((), (), s32[]{:S(2)}) async-start(), calls=%async_computation.1 | async-start | bytes 2949120 | tf_op jit(solution)/shard_map/all_gather | solution.py:188
  7.9 286.3 %all-gather.7.cloned.1.call-start = ((), (), s32[]{:S(2)}) async-start(), calls=%async_computation.2 | async-start | bytes 2949120 | tf_op jit(solution)/shard_map/all_gather | solution.py:241
  8.0 22.3 %collective-permute-start.6 = (bf16[384,768]{1,0:T(8,128)(2,1)}, bf16[384,768]{1,0:T(8,128)(2,1)}, u32[]{:S(2)}, u32[]{:S(2)}) collective-permute-start(bf16[384,768]{1,0:T(8,128)(2,1)} %bitcast.185), channel_id=1, source_target_pairs={{0,4},{4,8},{8,12},{12,0},{1,5},{5,9},{9,13},{13,1},{2,6},{6,10},{... | collective-permute-start | bytes 1769480 | tf_op jit(solution)/shard_map/ppermute | solution.py:33
  11.0 61.8 %collective-permute-start.7 = (bf16[384,768]{1,0:T(8,128)(2,1)}, bf16[384,768]{1,0:T(8,128)(2,1)}, u32[]{:S(2)}, u32[]{:S(2)}) collective-permute-start(bf16[384,768]{1,0:T(8,128)(2,1)} %bitcast.186), channel_id=1, source_target_pairs={{0,12},{4,0},{8,4},{12,8},{1,13},{5,1},{9,5},{13,9},{2,14},{6,2},{... | collective-permute-start | bytes 1769480 | tf_op jit(solution)/shard_map/ppermute | solution.py:38
  30.3 49.8 %collective-permute-start.8 = (bf16[384,768]{1,0:T(8,128)(2,1)}, bf16[384,768]{1,0:T(8,128)(2,1)}, u32[]{:S(2)}, u32[]{:S(2)}) collective-permute-start(bf16[384,768]{1,0:T(8,128)(2,1)} %collective-permute-done.6), channel_id=1, source_target_pairs={{0,4},{4,8},{8,12},{12,0},{1,5},{5,9},{9,13},{13,1},{2,6},{6,10},{... | collective-permute-start | bytes 1769480 | tf_op jit(solution)/shard_map/ppermute | solution.py:33
  40.5 518.0 %all-reduce.6.cloned.1.call-start = ((), (), s32[]{:S(2)}) async-start(), calls=%async_computation | async-start | bytes 301056 | tf_op jit(solution)/shard_map/psum | solution.py:306
  101.3 10.2 %collective-permute-start.1 = (bf16[3,16,768]{2,1,0:T(8,128)(2,1)S(1)}, bf16[3,16,768]{2,1,0:T(8,128)(2,1)S(1)}, u32[]{:S(2)}, u32[]{:S(2)}) collective-permute-start(bf16[3,16,768]{2,1,0:T(8,128)(2,1)S(1)} %get-tuple-element.1228), channel_id=1, source_target_pairs={{4,0},{8,4},{12,8},{5,1},{9,5},{13,9},{6,2},{10,6},{14,10},{7,3},{... | collective-permute-start | bytes 221192 | tf_op jit(solution)/shard_map/while/body/eval_jaxpr/ppermute | solution.py:63
  102.6 8.9 %collective-permute-start.2 = (bf16[3,16,768]{2,1,0:T(8,128)(2,1)S(1)}, bf16[3,16,768]{2,1,0:T(8,128)(2,1)S(1)}, u32[]{:S(2)}, u32[]{:S(2)}) collective-permute-start(bf16[3,16,768]{2,1,0:T(8,128)(2,1)S(1)} %get-tuple-element.1229), channel_id=1, source_target_pairs={{0,4},{4,8},{8,12},{1,5},{5,9},{9,13},{2,6},{6,10},{10,14},{3,7},{... | collective-permute-start | bytes 221192 | tf_op jit(solution)/shard_map/while/body/eval_jaxpr/ppermute | solution.py:60
  136.9 6.7 %collective-permute-start.2 = (bf16[3,16,768]{2,1,0:T(8,128)(2,1)S(1)}, bf16[3,16,768]{2,1,0:T(8,128)(2,1)S(1)}, u32[]{:S(2)}, u32[]{:S(2)}) collective-permute-start(bf16[3,16,768]{2,1,0:T(8,128)(2,1)S(1)} %get-tuple-element.1229), channel_id=1, source_target_pairs={{0,4},{4,8},{8,12},{1,5},{5,9},{9,13},{2,6},{6,10},{10,14},{3,7},{... | collective-permute-start | bytes 221192 | tf_op jit(solution)/shard_map/while/body/eval_jaxpr/ppermute | solution.py:60
  168.9 6.9 %collective-permute-start.2 = (bf16[3,16,768]{2,1,0:T(8,128)(2,1)S(1)}, bf16[3,16,768]{2,1,0:T(8,128)(2,1)S(1)}, u32[]{:S(2)}, u32[]{:S(2)}) collective-permute-start(bf16[3,16,768]{2,1,0:T(8,128)(2,1)S(1)} %get-tuple-element.1229), channel_id=1, source_target_pairs={{0,4},{4,8},{8,12},{1,5},{5,9},{9,13},{2,6},{6,10},{10,14},{3,7},{... | collective-permute-start | bytes 221192 | tf_op jit(solution)/shard_map/while/body/eval_jaxpr/ppermute | solution.py:60
  201.1 6.9 %collective-permute-start.2 = (bf16[3,16,768]{2,1,0:T(8,128)(2,1)S(1)}, bf16[3,16,768]{2,1,0:T(8,128)(2,1)S(1)}, u32[]{:S(2)}, u32[]{:S(2)}) collective-permute-start(bf16[3,16,768]{2,1,0:T(8,128)(2,1)S(1)} %get-tuple-element.1229), channel_id=1, source_target_pairs={{0,4},{4,8},{8,12},{1,5},{5,9},{9,13},{2,6},{6,10},{10,14},{3,7},{... | collective-permute-start | bytes 221192 | tf_op jit(solution)/shard_map/while/body/eval_jaxpr/ppermute | solution.py:60
  243.0 25.8 %collective-permute-start = (bf16[4,16,768]{2,1,0:T(8,128)(2,1)}, bf16[4,16,768]{2,1,0:T(8,128)(2,1)S(1)}, u32[]{:S(2)}, u32[]{:S(2)}) collective-permute-start(bf16[4,16,768]{2,1,0:T(8,128)(2,1)} %get-tuple-element.1363), channel_id=1, source_target_pairs={{0,1},{1,2},{2,3},{4,5},{5,6},{6,7},{8,9},{9,10},{10,11},{12,13},{... | collective-permute-start | bytes 294920 | tf_op jit(solution)/shard_map/while/body/eval_jaxpr/ppermute | solution.py:52
  294.3 24.8 %collective-permute-start.3 = (bf16[4,16,768]{2,1,0:T(8,128)(2,1)S(1)}, bf16[4,16,768]{2,1,0:T(8,128)(2,1)S(1)}, u32[]{:S(2)}, u32[]{:S(2)}) collective-permute-start(bf16[4,16,768]{2,1,0:T(8,128)(2,1)S(1)} %broadcast_select_fusion.4), channel_id=1, source_target_pairs={{1,0},{2,1},{3,2},{5,4},{6,5},{7,6},{9,8},{10,9},{11,10},{13,12},{... | collective-permute-start | bytes 294920 | tf_op jit(solution)/shard_map/while/body/eval_jaxpr/ppermute | solution.py:52
  320.1 7.1 %collective-permute-start.4 = (bf16[3,16,768]{2,1,0:T(8,128)(2,1)S(1)}, bf16[3,16,768]{2,1,0:T(8,128)(2,1)S(1)}, u32[]{:S(2)}, u32[]{:S(2)}) collective-permute-start(bf16[3,16,768]{2,1,0:T(8,128)(2,1)S(1)} %get-tuple-element.1258), channel_id=1, source_target_pairs={{4,0},{8,4},{12,8},{5,1},{9,5},{13,9},{6,2},{10,6},{14,10},{7,3},{... | collective-permute-start | bytes 221192 | tf_op jit(solution)/shard_map/while/body/eval_jaxpr/ppermute | solution.py:63
  329.4 6.8 %collective-permute-start.3 = (bf16[4,16,768]{2,1,0:T(8,128)(2,1)S(1)}, bf16[4,16,768]{2,1,0:T(8,128)(2,1)S(1)}, u32[]{:S(2)}, u32[]{:S(2)}) collective-permute-start(bf16[4,16,768]{2,1,0:T(8,128)(2,1)S(1)} %broadcast_select_fusion.4), channel_id=1, source_target_pairs={{1,0},{2,1},{3,2},{5,4},{6,5},{7,6},{9,8},{10,9},{11,10},{13,12},{... | collective-permute-start | bytes 294920 | tf_op jit(solution)/shard_map/while/body/eval_jaxpr/ppermute | solution.py:52
  337.2 7.1 %collective-permute-start.4 = (bf16[3,16,768]{2,1,0:T(8,128)(2,1)S(1)}, bf16[3,16,768]{2,1,0:T(8,128)(2,1)S(1)}, u32[]{:S(2)}, u32[]{:S(2)}) collective-permute-start(bf16[3,16,768]{2,1,0:T(8,128)(2,1)S(1)} %get-tuple-element.1258), channel_id=1, source_target_pairs={{4,0},{8,4},{12,8},{5,1},{9,5},{13,9},{6,2},{10,6},{14,10},{7,3},{... | collective-permute-start | bytes 221192 | tf_op jit(solution)/shard_map/while/body/eval_jaxpr/ppermute | solution.py:63
  346.5 17.8 %collective-permute-start.3 = (bf16[4,16,768]{2,1,0:T(8,128)(2,1)S(1)}, bf16[4,16,768]{2,1,0:T(8,128)(2,1)S(1)}, u32[]{:S(2)}, u32[]{:S(2)}) collective-permute-start(bf16[4,16,768]{2,1,0:T(8,128)(2,1)S(1)} %broadcast_select_fusion.4), channel_id=1, source_target_pairs={{1,0},{2,1},{3,2},{5,4},{6,5},{7,6},{9,8},{10,9},{11,10},{13,12},{... | collective-permute-start | bytes 294920 | tf_op jit(solution)/shard_map/while/body/eval_jaxpr/ppermute | solution.py:52
  365.4 7.1 %collective-permute-start.4 = (bf16[3,16,768]{2,1,0:T(8,128)(2,1)S(1)}, bf16[3,16,768]{2,1,0:T(8,128)(2,1)S(1)}, u32[]{:S(2)}, u32[]{:S(2)}) collective-permute-start(bf16[3,16,768]{2,1,0:T(8,128)(2,1)S(1)} %get-tuple-element.1258), channel_id=1, source_target_pairs={{4,0},{8,4},{12,8},{5,1},{9,5},{13,9},{6,2},{10,6},{14,10},{7,3},{... | collective-permute-start | bytes 221192 | tf_op jit(solution)/shard_map/while/body/eval_jaxpr/ppermute | solution.py:63
  374.7 39.3 %collective-permute-start.3 = (bf16[4,16,768]{2,1,0:T(8,128)(2,1)S(1)}, bf16[4,16,768]{2,1,0:T(8,128)(2,1)S(1)}, u32[]{:S(2)}, u32[]{:S(2)}) collective-permute-start(bf16[4,16,768]{2,1,0:T(8,128)(2,1)S(1)} %broadcast_select_fusion.4), channel_id=1, source_target_pairs={{1,0},{2,1},{3,2},{5,4},{6,5},{7,6},{9,8},{10,9},{11,10},{13,12},{... | collective-permute-start | bytes 294920 | tf_op jit(solution)/shard_map/while/body/eval_jaxpr/ppermute | solution.py:52
  426.6 7.1 %collective-permute-start.4 = (bf16[3,16,768]{2,1,0:T(8,128)(2,1)S(1)}, bf16[3,16,768]{2,1,0:T(8,128)(2,1)S(1)}, u32[]{:S(2)}, u32[]{:S(2)}) collective-permute-start(bf16[3,16,768]{2,1,0:T(8,128)(2,1)S(1)} %get-tuple-element.1258), channel_id=1, source_target_pairs={{4,0},{8,4},{12,8},{5,1},{9,5},{13,9},{6,2},{10,6},{14,10},{7,3},{... | collective-permute-start | bytes 221192 | tf_op jit(solution)/shard_map/while/body/eval_jaxpr/ppermute | solution.py:63
  455.1 7.1 %collective-permute-start.4 = (bf16[3,16,768]{2,1,0:T(8,128)(2,1)S(1)}, bf16[3,16,768]{2,1,0:T(8,128)(2,1)S(1)}, u32[]{:S(2)}, u32[]{:S(2)}) collective-permute-start(bf16[3,16,768]{2,1,0:T(8,128)(2,1)S(1)} %get-tuple-element.1258), channel_id=1, source_target_pairs={{4,0},{8,4},{12,8},{5,1},{9,5},{13,9},{6,2},{10,6},{14,10},{7,3},{... | collective-permute-start | bytes 221192 | tf_op jit(solution)/shard_map/while/body/eval_jaxpr/ppermute | solution.py:63
  464.3 6.7 %collective-permute-start.3 = (bf16[4,16,768]{2,1,0:T(8,128)(2,1)S(1)}, bf16[4,16,768]{2,1,0:T(8,128)(2,1)S(1)}, u32[]{:S(2)}, u32[]{:S(2)}) collective-permute-start(bf16[4,16,768]{2,1,0:T(8,128)(2,1)S(1)} %broadcast_select_fusion.4), channel_id=1, source_target_pairs={{1,0},{2,1},{3,2},{5,4},{6,5},{7,6},{9,8},{10,9},{11,10},{13,12},{... | collective-permute-start | bytes 294920 | tf_op jit(solution)/shard_map/while/body/eval_jaxpr/ppermute | solution.py:52
  483.6 7.1 %collective-permute-start.4 = (bf16[3,16,768]{2,1,0:T(8,128)(2,1)S(1)}, bf16[3,16,768]{2,1,0:T(8,128)(2,1)S(1)}, u32[]{:S(2)}, u32[]{:S(2)}) collective-permute-start(bf16[3,16,768]{2,1,0:T(8,128)(2,1)S(1)} %get-tuple-element.1258), channel_id=1, source_target_pairs={{4,0},{8,4},{12,8},{5,1},{9,5},{13,9},{6,2},{10,6},{14,10},{7,3},{... | collective-permute-start | bytes 221192 | tf_op jit(solution)/shard_map/while/body/eval_jaxpr/ppermute | solution.py:63
  511.8 7.1 %collective-permute-start.4 = (bf16[3,16,768]{2,1,0:T(8,128)(2,1)S(1)}, bf16[3,16,768]{2,1,0:T(8,128)(2,1)S(1)}, u32[]{:S(2)}, u32[]{:S(2)}) collective-permute-start(bf16[3,16,768]{2,1,0:T(8,128)(2,1)S(1)} %get-tuple-element.1258), channel_id=1, source_target_pairs={{4,0},{8,4},{12,8},{5,1},{9,5},{13,9},{6,2},{10,6},{14,10},{7,3},{... | collective-permute-start | bytes 221192 | tf_op jit(solution)/shard_map/while/body/eval_jaxpr/ppermute | solution.py:63
  (35 other events, 215.5 us)
Sparse Core Ops, SparseCore 0:
  9.6 80.5 all-gather.4
  91.8 51.8 all-gather.6
  522.0 36.4 all-reduce.5
